TPU v7x, 32 devices: a whole 2x2x4 slice. The times are simulated.
32 devices in a mesh: layer: 16 (over z, y, core), rhs: 2 (over x).
Axes of the slice: x: 2, y: 2, z: 4, core: 2. Of those that a mesh axis runs over, the one named last changes fastest.
Arguments:
- diag_block: float32 [32, 384, 384], P('layer'), may hold values from -0.234742767 to 4.6347428, as said below
- coupling: float32 [32, 384, 384], P('layer'), may hold values from -1.76123724 to 1.76123724
- right_side: float32 [32, 384, 256], P('layer', None, 'rhs'), may hold values from -6 to 6
Outputs:
- inverse_out: float32 [32, 384, 384], P('layer')
- rhs_out: float32 [32, 384, 256], P('layer', None, 'rhs')
Inputs may be any that keep to these rules, and one draw needn't show every extreme that they name: `diag_block`: each diagonal block is symmetric.
All inputs are finite; a program needn't handle non-finite values.
Results may differ from a plain program's by a relative error of at most 0.00013.
Values sent between devices are 32-bit elements; how exact they have to be, the bound alone decides.
A program may use at most 64 MiB of HBM per device.

v0:
```python
import jax
import jax.numpy as jnp
from jax import lax
from jax.sharding import PartitionSpec as P

LEVELS = 3


def passed_along(block, axis, distance):
    devices = range(lax.axis_size(axis))
    route = [((i - distance) % len(devices), i) for i in devices]
    return lax.ppermute(block, axis, route)


def matmul(first, second):
    return jnp.dot(
        first, second, precision=lax.Precision.HIGH, preferred_element_type=jnp.float32
    )


def invert(block_now):
    orbitals = block_now.shape[0]
    identity = jnp.eye(orbitals, dtype=jnp.float32)
    scale = orbitals / jnp.trace(block_now)
    err = identity - scale * block_now
    square = matmul(err, err)
    approx = scale * (identity + err)
    approx = approx + matmul(approx, square)
    return approx + matmul(approx, matmul(square, square))


def prepare(operands):
    approx, u_self, r_self = operands
    solved = matmul(approx, jnp.concatenate([u_self, r_self], axis=1))
    return (solved, matmul(u_self.T, solved))


def prepare_skip(operands):
    approx, u_self, r_self = operands
    width = u_self.shape[1] + r_self.shape[1]
    empty = jnp.zeros((approx.shape[0], width), jnp.float32)
    return (empty, empty)


def eliminate(operands):
    diag_now, u_self, r_self = operands
    approx = invert(diag_now)
    solved, right_part = prepare((approx, u_self, r_self))
    return (approx, solved, right_part)


def eliminate_skip(operands):
    diag_now, u_self, r_self = operands
    solved, right_part = prepare_skip((diag_now, u_self, r_self))
    return (jnp.zeros_like(diag_now), solved, right_part)


def complete(operands):
    u_left, approx, solved = operands
    first = matmul(approx, u_left.T)
    return matmul(u_left, jnp.concatenate([first, solved], axis=1))


def complete_skip(operands):
    u_left, approx, solved = operands
    return jnp.zeros((u_left.shape[0], u_left.shape[1] + solved.shape[1]), jnp.float32)


def lift(first, second, stride):
    return passed_along((first, second), "layer", stride)


def send_down(left_part, stride, blocks):
    orbitals = left_part.shape[0]
    columns = blocks * orbitals
    head = left_part[:, :columns]
    tail = left_part[:, 2 * orbitals :]
    head_in, tail_in = passed_along((head, tail), "layer", -stride)
    return (head_in, tail_in)


def body(diag_block, coupling, right_side):
    orbitals = diag_block.shape[1]
    position = lax.axis_index("layer")
    low_diag, high_diag = (diag_block[0], diag_block[1])
    low_coup, high_coup = (coupling[0], coupling[1])
    low_rhs, high_rhs = (right_side[0], right_side[1])
    low_inverse = invert(low_diag)
    solved, right_part = prepare((low_inverse, low_coup, low_rhs))
    first_in, second_in = lift(high_coup, jnp.zeros_like(high_rhs), 1)
    left_part = complete((first_in, low_inverse, solved))
    head_in, tail_in = send_down(left_part, 1, 2)
    high_diag = high_diag - head_in[:, :orbitals] - right_part[:, :orbitals]
    high_coup = -head_in[:, orbitals : 2 * orbitals]
    high_rhs = high_rhs - tail_in - right_part[:, orbitals:]
    high_inverse = jnp.zeros_like(high_diag)
    high_record = jnp.zeros_like(high_rhs)
    for level_num in range(1, LEVELS):
        stride = 2 ** (level_num - 1)
        phase = (position + 1) % (2 * stride)
        removed = phase == stride
        survive = phase == 0
        approx, solved, right_part = lax.cond(
            removed, eliminate, eliminate_skip, (high_diag, high_coup, high_rhs)
        )
        first = jnp.where(removed, right_part[:, :orbitals], high_coup)
        second = jnp.where(removed, right_part[:, orbitals:], jnp.zeros_like(high_rhs))
        first_in, second_in = lift(first, second, stride)
        left_part = lax.cond(removed, complete, complete_skip, (first_in, approx, solved))
        blocks = 2 if level_num < LEVELS - 1 else 1
        head_in, tail_in = send_down(left_part, stride, blocks)
        high_inverse = jnp.where(removed, approx, high_inverse)
        high_record = jnp.where(removed, high_rhs, high_record)
        high_diag = jnp.where(survive, high_diag - head_in[:, :orbitals] - first_in, high_diag)
        high_rhs = jnp.where(survive, high_rhs - tail_in - second_in, high_rhs)
        if blocks == 2:
            high_coup = jnp.where(survive, -head_in[:, orbitals : 2 * orbitals], high_coup)
    final_keep = (position + 1) % 2 ** (LEVELS - 1) == 0
    final_inverse = lax.cond(final_keep, invert, jnp.zeros_like, high_diag)
    high_inverse = jnp.where(final_keep, final_inverse, high_inverse)
    high_record = jnp.where(final_keep, high_rhs, high_record)
    inverse_out = jnp.stack([low_inverse, high_inverse], axis=0)
    rhs_out = jnp.stack([low_rhs, high_record], axis=0)
    return (inverse_out, rhs_out)


def solution(mesh):
    return jax.shard_map(
        body,
        mesh=mesh,
        in_specs=(P("layer", None, None), P("layer", None, None), P("layer", None, "rhs")),
        out_specs=(P("layer", None, None), P("layer", None, "rhs")),
        check_vma=False,
    )
```

profile of v0, /device:TPU:5, one launch (start us, length us, event | category | flops | bytes accessed | tf_op | source)
XLA Modules:
  0.0 144.6 jit_solution(10674204822691201056)
XLA Ops:
  0.6 2.2 %slice_bitcast_fusion.1 = (f32[384,384]{1,0:T(8,128)}, f32[384,384]{1,0:T(8,128)S(1)}) fusion(f32[2,384,384]{2,1,0:T(8,128)} %param.14), kind=kLoop, calls=%fused_computation.82 | loop fusion | bytes 2359296 | tf_op jit(solution)/shard_map/squeeze | solution.py:86
  2.9 1.8 %collective-permute-start = (f32[384,384]{1,0:T(8,128)}, f32[384,384]{1,0:T(8,128)S(1)}, u32[]{:S(2)}, u32[]{:S(2)}) collective-permute-start(f32[384,384]{1,0:T(8,128)} %get-tuple-element.124), channel_id=1, source_target_pairs={{30,0},{0,2},{2,4},{4,6},{6,8},{8,10},{10,12},{12,14},{14,16},{16,... | collective-permute-start | bytes 1769480 | tf_op jit(solution)/shard_map/ppermute | solution.py:12
  13.4 2.4 %convolution_bitcast_fusion.4 = f32[384,896]{1,0:T(8,128)S(1)} fusion(f32[384,384]{1,0:T(8,128)} %copy-done.7, f32[384,512]{1,0:T(8,128)S(1)} %fusion.36, f32[384,384]{1,0:T(8,128)S(1)} %fusion.65), kind=kOutput, calls=%fused_computation.53 | convolution fusion | flops 793067520 | bytes 3342336 | tf_op jit(solution)/shard_map/dot_general | solution.py:16
  18.2 2.0 %convolution_bitcast_fusion.5 = f32[384,512]{1,0:T(8,128)S(1)} fusion(f32[384,512]{1,0:T(8,128)S(1)} %fusion.36, f32[2,384,384]{2,1,0:T(8,128)} %param.14), kind=kOutput, calls=%fused_computation.59 | convolution fusion | flops 452984832 | bytes 2162688 | tf_op jit(solution)/shard_map/dot_general | solution.py:16
  20.2 16.1 %collective-permute-done.2 = f32[384,128]{1,0:T(8,128)S(1)} collective-permute-done((f32[384,128]{1,0:T(8,128)S(1)}, f32[384,128]{1,0:T(8,128)S(1)}, u32[]{:S(2)}, u32[]{:S(2)}) %collective-permute-start.2) | collective-permute-done | bytes 196640 | tf_op jit(solution)/shard_map/ppermute | solution.py:12
  37.8 2.1 %conditional.5 = (f32[384,384]{1,0:T(8,128)S(1)}, f32[384,512]{1,0:T(8,128)}, f32[384,384]{1,0:T(8,128)}, f32[384,128]{1,0:T(8,128)S(1)}) conditional(s32[]{:T(128)} %convert_element_type.46, () %tuple.57, (f32[384,384]{1,0:T(8,128)S(1)}, f32[384,384]{1,0:T(8,128)S(1)}, f32[384,128]{1,0:T(8,128)S(1)}) %tuple.58), branch_computations={%region_1.2_spmd, %region_2.4_spmd} | conditional | flops 2267332608 | bytes 18677872 | solution.py:103
  41.1 7.5 %collective-permute-start.3 = (f32[384,384]{1,0:T(8,128)S(1)}, f32[384,384]{1,0:T(8,128)}, u32[]{:S(2)}, u32[]{:S(2)}) collective-permute-start(f32[384,384]{1,0:T(8,128)S(1)} %broadcast_select_fusion.1), channel_id=1, source_target_pairs={{30,0},{0,2},{2,4},{4,6},{6,8},{8,10},{10,12},{12,14},{14,16},{16,... | collective-permute-start | bytes 1769480 | tf_op jit(solution)/shard_map/ppermute | solution.py:12
  48.6 6.8 %collective-permute-done.3 = f32[384,384]{1,0:T(8,128)} collective-permute-done((f32[384,384]{1,0:T(8,128)S(1)}, f32[384,384]{1,0:T(8,128)}, u32[]{:S(2)}, u32[]{:S(2)}) %collective-permute-start.3) | collective-permute-done | bytes 589856 | tf_op jit(solution)/shard_map/ppermute | solution.py:12
  56.6 2.7 %copy.27 = f32[384,768]{1,0:T(8,128)} copy(f32[384,768]{0,1:T(8,128)} %slice.114) | data formatting | bytes 2359296
  59.3 5.9 %collective-permute-start.4 = (f32[384,768]{1,0:T(8,128)}, f32[384,768]{1,0:T(8,128)}, u32[]{:S(2)}, u32[]{:S(2)}) collective-permute-start(f32[384,768]{1,0:T(8,128)} %copy.27), channel_id=1, source_target_pairs={{2,0},{4,2},{6,4},{8,6},{10,8},{12,10},{14,12},{16,14},{18,16},{20... | collective-permute-start | bytes 3538952 | tf_op jit(solution)/shard_map/ppermute | solution.py:12
  65.9 2.9 %collective-permute-start.6 = (f32[384,128]{1,0:T(8,128)}, f32[384,128]{1,0:T(8,128)}, u32[]{:S(2)}, u32[]{:S(2)}) collective-permute-start(f32[384,128]{1,0:T(8,128)} %broadcast_select_fusion.3), channel_id=1, source_target_pairs={{30,0},{0,2},{2,4},{4,6},{6,8},{8,10},{10,12},{12,14},{14,16},{16,... | collective-permute-start | bytes 589832 | tf_op jit(solution)/shard_map/ppermute | solution.py:12
  69.0 2.7 %collective-permute-done.6 = f32[384,128]{1,0:T(8,128)} collective-permute-done((f32[384,128]{1,0:T(8,128)}, f32[384,128]{1,0:T(8,128)}, u32[]{:S(2)}, u32[]{:S(2)}) %collective-permute-start.6) | collective-permute-done | bytes 196640 | tf_op jit(solution)/shard_map/ppermute | solution.py:12
  71.8 12.6 %collective-permute-done.5 = f32[384,128]{1,0:T(8,128)S(1)} collective-permute-done((f32[384,128]{1,0:T(8,128)S(1)}, f32[384,128]{1,0:T(8,128)S(1)}, u32[]{:S(2)}, u32[]{:S(2)}) %collective-permute-start.5) | collective-permute-done | bytes 196640 | tf_op jit(solution)/shard_map/ppermute | solution.py:12
  85.4 1.7 %fusion.42 = (f32[384,384]{1,0:T(8,128)S(1)}, f32[384,384]{1,0:T(8,128)S(1)}) fusion(f32[384,768]{1,0:T(8,128)} %collective-permute-done.4, pred[]{:T(512)S(6)} %eq.65, f32[384,768]{1,0:T(8,128)} %collective-permute-done.1, f32[384,384]{1,0:T(8,128)S(1)} %get-tuple-element.123, f32[384,384]{1,0:T(8,128)} %collective-permute-done.3), kind=kLoop, calls=%fused_computation.68 | loop fusion | flops 884736 | bytes 4128769 | tf_op jit(solution)/shard_map/jit(_where)/select_n | solution.py:117
  87.1 2.6 %conditional.7 = (f32[384,384]{1,0:T(8,128)S(1)}, f32[384,512]{1,0:T(8,128)}, f32[384,384]{1,0:T(8,128)}, f32[384,128]{1,0:T(8,128)}) conditional(s32[]{:T(128)} %convert_element_type.47, () %tuple.61, (f32[384,384]{1,0:T(8,128)S(1)}, f32[384,384]{1,0:T(8,128)S(1)}, f32[384,128]{1,0:T(8,128)S(1)}) %tuple.62), branch_computations={%region_6.7_spmd, %region_7.9_spmd} | conditional | flops 2267332608 | bytes 22020260 | solution.py:103
  89.8 13.8 %collective-permute-start.7 = (f32[384,384]{1,0:T(8,128)S(1)}, f32[384,384]{1,0:T(8,128)S(1)}, u32[]{:S(2)}, u32[]{:S(2)}) collective-permute-start(f32[384,384]{1,0:T(8,128)S(1)} %broadcast_select_fusion), channel_id=1, source_target_pairs={{28,0},{30,2},{0,4},{2,6},{4,8},{6,10},{8,12},{10,14},{12,16},{14,... | collective-permute-start | bytes 1769480 | tf_op jit(solution)/shard_map/ppermute | solution.py:12
  103.6 6.8 %collective-permute-done.7 = f32[384,384]{1,0:T(8,128)S(1)} collective-permute-done((f32[384,384]{1,0:T(8,128)S(1)}, f32[384,384]{1,0:T(8,128)S(1)}, u32[]{:S(2)}, u32[]{:S(2)}) %collective-permute-start.7) | collective-permute-done | bytes 589856 | tf_op jit(solution)/shard_map/ppermute | solution.py:12
  111.6 1.9 %slice.118 = f32[384,384]{0,1:T(8,128)} slice(f32[384,896]{0,1:T(8,128)} %get-tuple-element.145), slice={[0:384], [0:384]} | slice | bytes 1179648 | tf_op jit(solution)/shard_map/slice | solution.py:76
  113.5 2.1 %copy.29 = f32[384,384]{1,0:T(8,128)} copy(f32[384,384]{0,1:T(8,128)} %slice.118) | data formatting | bytes 1179648
  115.6 8.3 %collective-permute-start.8 = (f32[384,384]{1,0:T(8,128)}, f32[384,384]{1,0:T(8,128)}, u32[]{:S(2)}, u32[]{:S(2)}) collective-permute-start(f32[384,384]{1,0:T(8,128)} %copy.29), channel_id=1, source_target_pairs={{4,0},{6,2},{8,4},{10,6},{12,8},{14,10},{16,12},{18,14},{20,16},{2... | collective-permute-start | bytes 1769480 | tf_op jit(solution)/shard_map/ppermute | solution.py:12
  127.9 6.6 %collective-permute-done.10 = f32[384,128]{1,0:T(8,128)} collective-permute-done((f32[384,128]{1,0:T(8,128)}, f32[384,128]{1,0:T(8,128)}, u32[]{:S(2)}, u32[]{:S(2)}) %collective-permute-start.10) | collective-permute-done | bytes 196640 | tf_op jit(solution)/shard_map/ppermute | solution.py:12
  136.4 1.7 %pad_maximum_fusion.1 = f32[2,384,128]{2,1,0:T(8,128)} fusion(f32[1,384,128]{2,1,0:T(8,128)S(1)} %select_bitcast_fusion.1, f32[1,384,128]{2,1,0:T(8,128)} %get-tuple-element.126), kind=kLoop, calls=%fused_computation.91 | loop fusion | flops 98304 | bytes 786432 | tf_op jit(solution)/shard_map/stack | solution.py:123
  138.1 5.3 %conditional.9 = (f32[384,384]{1,0:T(8,128)S(1)}) conditional(s32[]{:T(128)} %convert_element_type.45, () %tuple.55, (pred[]{:T(512)}, f32[384,384]{1,0:T(8,128)S(1)}, f32[384,384]{1,0:T(8,128)}, f32[384,384]{1,0:T(8,128)S(1)}) %tuple.64), branch_computations={%region_11.12_spmd, %region_12.14_spmd} | conditional | flops 1361608704 | bytes 8257569 | solution.py:119
  138.1 1.8 %select_reduce_fusion.2 = (f32[]{:T(128)}, f32[384,384]{1,0:T(8,128)S(1)}) fusion(f32[384,384]{1,0:T(8,128)S(1)} %get-tuple-element.85, f32[384,384]{1,0:T(8,128)S(1)} %get-tuple-element.87, f32[384,384]{1,0:T(8,128)} %get-tuple-element.86, pred[]{:T(512)} %get-tuple-element.84), kind=kLoop, calls=%fused_computation.47 | loop fusion | flops 884735 | bytes 2359301 | tf_op jit(solution)/shard_map/cond/branch_1_fun/jit(trace)/reduce_sum | solution.py:24
  (61 shorter events, 32.9 us)
Async XLA Ops:
  0.6 4.0 %copy-start.4 = (f32[2,384,384]{2,1,0:T(8,128)S(1)}, f32[2,384,384]{2,1,0:T(8,128)}, u32[]{:S(2)}) copy-start(f32[2,384,384]{2,1,0:T(8,128)} %param.13) | copy-start | bytes 3538948
  2.9 8.9 %collective-permute-start = (f32[384,384]{1,0:T(8,128)}, f32[384,384]{1,0:T(8,128)S(1)}, u32[]{:S(2)}, u32[]{:S(2)}) collective-permute-start(f32[384,384]{1,0:T(8,128)} %get-tuple-element.124), channel_id=1, source_target_pairs={{30,0},{0,2},{2,4},{4,6},{6,8},{8,10},{10,12},{12,14},{14,16},{16,... | collective-permute-start | bytes 1769480 | tf_op jit(solution)/shard_map/ppermute | solution.py:12
  7.5 1.0 copy-start.8
  11.8 0.8 copy-start.7
  16.9 19.5 %collective-permute-start.1 = (f32[384,768]{1,0:T(8,128)}, f32[384,768]{1,0:T(8,128)}, u32[]{:S(2)}, u32[]{:S(2)}) collective-permute-start(f32[384,768]{1,0:T(8,128)} %slice.108), channel_id=1, source_target_pairs={{2,0},{4,2},{6,4},{8,6},{10,8},{12,10},{14,12},{16,14},{18,16},{20... | collective-permute-start | bytes 3538952 | tf_op jit(solution)/shard_map/ppermute | solution.py:12
  18.1 18.2 %copy-start.9 = (f32[2,384,128]{2,1,0:T(8,128)S(1)}, f32[2,384,128]{2,1,0:T(8,128)}, u32[]{:S(2)}) copy-start(f32[2,384,128]{2,1,0:T(8,128)} %param.15) | copy-start | bytes 1179652
  18.1 18.3 %copy-start.5 = (f32[2,384,384]{2,1,0:T(8,128)S(1)}, f32[2,384,384]{2,1,0:T(8,128)}, u32[]{:S(2)}) copy-start(f32[2,384,384]{2,1,0:T(8,128)} %param.13) | copy-start | bytes 3538948
  18.2 18.2 %collective-permute-start.2 = (f32[384,128]{1,0:T(8,128)S(1)}, f32[384,128]{1,0:T(8,128)S(1)}, u32[]{:S(2)}, u32[]{:S(2)}) collective-permute-start(f32[384,128]{1,0:T(8,128)S(1)} %slice.112), channel_id=1, source_target_pairs={{2,0},{4,2},{6,4},{8,6},{10,8},{12,10},{14,12},{16,14},{18,16},{20... | collective-permute-start | bytes 589832 | tf_op jit(solution)/shard_map/ppermute | solution.py:12
  41.1 14.3 %collective-permute-start.3 = (f32[384,384]{1,0:T(8,128)S(1)}, f32[384,384]{1,0:T(8,128)}, u32[]{:S(2)}, u32[]{:S(2)}) collective-permute-start(f32[384,384]{1,0:T(8,128)S(1)} %broadcast_select_fusion.1), channel_id=1, source_target_pairs={{30,0},{0,2},{2,4},{4,6},{6,8},{8,10},{10,12},{12,14},{14,16},{16,... | collective-permute-start | bytes 1769480 | tf_op jit(solution)/shard_map/ppermute | solution.py:12
  59.3 26.1 %collective-permute-start.4 = (f32[384,768]{1,0:T(8,128)}, f32[384,768]{1,0:T(8,128)}, u32[]{:S(2)}, u32[]{:S(2)}) collective-permute-start(f32[384,768]{1,0:T(8,128)} %copy.27), channel_id=1, source_target_pairs={{2,0},{4,2},{6,4},{8,6},{10,8},{12,10},{14,12},{16,14},{18,16},{20... | collective-permute-start | bytes 3538952 | tf_op jit(solution)/shard_map/ppermute | solution.py:12
  65.9 5.9 %collective-permute-start.6 = (f32[384,128]{1,0:T(8,128)}, f32[384,128]{1,0:T(8,128)}, u32[]{:S(2)}, u32[]{:S(2)}) collective-permute-start(f32[384,128]{1,0:T(8,128)} %broadcast_select_fusion.3), channel_id=1, source_target_pairs={{30,0},{0,2},{2,4},{4,6},{6,8},{8,10},{10,12},{12,14},{14,16},{16,... | collective-permute-start | bytes 589832 | tf_op jit(solution)/shard_map/ppermute | solution.py:12
  68.9 15.5 %collective-permute-start.5 = (f32[384,128]{1,0:T(8,128)S(1)}, f32[384,128]{1,0:T(8,128)S(1)}, u32[]{:S(2)}, u32[]{:S(2)}) collective-permute-start(f32[384,128]{1,0:T(8,128)S(1)} %copy.28), channel_id=1, source_target_pairs={{2,0},{4,2},{6,4},{8,6},{10,8},{12,10},{14,12},{16,14},{18,16},{20... | collective-permute-start | bytes 589832 | tf_op jit(solution)/shard_map/ppermute | solution.py:12
  89.8 20.6 %collective-permute-start.7 = (f32[384,384]{1,0:T(8,128)S(1)}, f32[384,384]{1,0:T(8,128)S(1)}, u32[]{:S(2)}, u32[]{:S(2)}) collective-permute-start(f32[384,384]{1,0:T(8,128)S(1)} %broadcast_select_fusion), channel_id=1, source_target_pairs={{28,0},{30,2},{0,4},{2,6},{4,8},{6,10},{8,12},{10,14},{12,16},{14,... | collective-permute-start | bytes 1769480 | tf_op jit(solution)/shard_map/ppermute | solution.py:12
  115.6 22.4 %collective-permute-start.8 = (f32[384,384]{1,0:T(8,128)}, f32[384,384]{1,0:T(8,128)}, u32[]{:S(2)}, u32[]{:S(2)}) collective-permute-start(f32[384,384]{1,0:T(8,128)} %copy.29), channel_id=1, source_target_pairs={{4,0},{6,2},{8,4},{10,6},{12,8},{14,10},{16,12},{18,14},{20,16},{2... | collective-permute-start | bytes 1769480 | tf_op jit(solution)/shard_map/ppermute | solution.py:12
  124.7 9.8 %collective-permute-start.10 = (f32[384,128]{1,0:T(8,128)}, f32[384,128]{1,0:T(8,128)}, u32[]{:S(2)}, u32[]{:S(2)}) collective-permute-start(f32[384,128]{1,0:T(8,128)} %broadcast_select_fusion.2), channel_id=1, source_target_pairs={{28,0},{30,2},{0,4},{2,6},{4,8},{6,10},{8,12},{10,14},{12,16},{14,... | collective-permute-start | bytes 589832 | tf_op jit(solution)/shard_map/ppermute | solution.py:12
  126.4 8.9 %collective-permute-start.9 = (f32[384,128]{1,0:T(8,128)}, f32[384,128]{1,0:T(8,128)}, u32[]{:S(2)}, u32[]{:S(2)}) collective-permute-start(f32[384,128]{1,0:T(8,128)} %copy.30), channel_id=1, source_target_pairs={{4,0},{6,2},{8,4},{10,6},{12,8},{14,10},{16,12},{18,14},{20,16},{2... | collective-permute-start | bytes 589832 | tf_op jit(solution)/shard_map/ppermute | solution.py:12
where the time goes:
time: 145 us
  waiting for transfers between devices  53.7 us (37%)
  starting transfers between devices  43.1 us (30%)
  local copies, waits for them, and re-layouts  20.6 us (14%)
  other arithmetic  13.1 us (9%)
  matrix products  11.7 us (8%)
  between operations  1.56 us (1%)
    ppermute x11, waiting for transfers between devices, passed_along(): return lax.ppermute(block, axis, route)  53.7 us
    ppermute x11, starting transfers between devices, passed_along(): return lax.ppermute(block, axis, route)  43.1 us
    dot_general x12, matrix products, matmul(): jnp.dot(first, second, precision=lax.Precision.HIGH, preferred_element_ty...  11.7 us
    unnamed x14, local copies, waits for them, and re-layouts  6.81 us
    another operation x8, local copies, waits for them, and re-layouts  5.03 us
    slice x3, local copies, waits for them, and re-layouts, send_down(): head = left_part[:, :columns]  4.1 us
  transfers between devices with their start and end apart: 11, of which 8 were waited for; matrix products, arithmetic and copies ran while one was open for 10% of the time, Pallas kernels for 0%

commit v1 on v0

v1 whole, which is shorter than its diff:
```python
import functools

import jax
import jax.numpy as jnp
from jax import lax
from jax.experimental import pallas as pl
from jax.experimental.pallas import tpu as pltpu
from jax.sharding import PartitionSpec as P

LEVELS = 3
TILE = 128


def split(value):
    high = value.astype(jnp.bfloat16)
    return high, (value - high.astype(jnp.float32)).astype(jnp.bfloat16)


def matmul(first, second, transposed=False):
    dims = (((1,), (1 if transposed else 0,)), ((), ()))

    def one(a, b):
        return lax.dot_general(a, b, dims, preferred_element_type=jnp.float32)

    return one(first[0], second[0]) + (one(first[0], second[1]) + one(first[1], second[0]))


def invert(block):
    orbitals = block.shape[0]
    rows = lax.broadcasted_iota(jnp.int32, (orbitals, orbitals), 0)
    columns = lax.broadcasted_iota(jnp.int32, (orbitals, orbitals), 1)
    on_diag = rows == columns
    trace = jnp.sum(jnp.where(on_diag, block, 0.0), axis=(0, 1), keepdims=True)
    scale = orbitals / trace
    identity = jnp.where(on_diag, 1.0, 0.0)
    err = identity - scale * block
    err_parts = split(err)
    square = matmul(err_parts, err_parts)
    square_parts = split(square)
    rest = err + (square + matmul(err_parts, square_parts))
    fourth = matmul(square_parts, square_parts)
    return scale * (identity + (rest + (fourth + matmul(split(rest), split(fourth)))))


def kernel(size, d_ref, u_ref, r_ref, inv_ref, rec_ref, d_now, u_now, x_in, u_in, r_in,
           q_out, q_in, s_out, s_in, send_sem, recv_sem):
    me = lax.axis_index("layer")
    orbitals = d_ref.shape[1]
    tiles = orbitals // TILE

    def at(distance):
        return {"layer": lax.rem(me + distance + size, size)}

    strides = [2 ** level for level in range(LEVELS - 1)]
    partners = [sign * stride for stride in strides for sign in (1, -1)]
    barrier = pltpu.get_barrier_semaphore()
    for distance in partners:
        pl.semaphore_signal(barrier, inc=1, device_id=at(distance), device_id_type=pl.DeviceIdType.MESH)
    pl.semaphore_wait(barrier, len(partners))

    def remote(src, dst, level, slot, distance):
        return pltpu.make_async_remote_copy(
            src_ref=src, dst_ref=dst, send_sem=send_sem.at[level, slot],
            recv_sem=recv_sem.at[level, slot], device_id=at(distance),
            device_id_type=pl.DeviceIdType.MESH,
        )

    def triangle(src, dst, level, slot, distance):
        copies = []
        for i in range(tiles):
            part = (pl.ds(i * TILE, TILE), pl.ds(i * TILE, orbitals - i * TILE))
            copies.append(remote(src.at[part], dst.at[part], level, slot + i, distance))
        return copies

    def mirror(ref):
        for i in range(tiles):
            for j in range(i + 1, tiles):
                low, high = pl.ds(i * TILE, TILE), pl.ds(j * TILE, TILE)
                ref[high, low] = ref[low, high].T

    def operands(level, stride):
        src_u, src_r = (u_ref.at[0], r_ref.at[0]) if level == 0 else (u_now, rec_ref.at[1])
        copies = [remote(src_r, r_in.at[level], level, 1, -stride)]
        if level < LEVELS - 1:
            copies.append(remote(src_u, u_in.at[level], level, 0, -stride))
        return copies

    def inverse_copies(level, stride):
        return triangle(inv_ref.at[min(level, 1)], x_in.at[level], level, 2, -stride)

    def right_copies(level, stride):
        return triangle(q_out, q_in.at[level - 1], level, 2 + tiles, stride) + [
            remote(s_out, s_in.at[level - 1], level, 2 + 2 * tiles, stride)
        ]

    def right_part(approx, u_self, r_self):
        parts = split(approx)
        turned = split(u_self.T)
        return (
            matmul(turned, split(matmul(parts, split(u_self)))),
            matmul(turned, split(matmul(parts, split(r_self)))),
        )

    def complete(level, stride, u_left):
        for copy in operands(level, stride) + inverse_copies(level, stride):
            copy.wait_recv()
        mirror(x_in.at[level])
        left = split(u_left[...])
        through = split(matmul(left, split(x_in[level])))
        d_now[...] -= matmul(through, left, transposed=True)
        rec_ref[1] -= matmul(through, split(r_in[level]))
        if level < LEVELS - 1:
            u_now[...] = -matmul(through, split(u_in[level]))

    first_level = operands(0, 1)
    for copy in first_level:
        copy.start()
    rec_ref[0] = r_ref[0]
    inv_ref[0] = invert(d_ref[0])
    for copy in inverse_copies(0, 1):
        copy.start()
    q_diag, q_rhs = right_part(inv_ref[0], u_ref[0], r_ref[0])
    d_now[...] = d_ref[1] - q_diag
    rec_ref[1] = r_ref[1] - q_rhs
    complete(0, 1, u_ref.at[1])

    for level in range(1, LEVELS):
        stride = 2 ** (level - 1)
        phase = lax.rem(me + 1, 2 * stride)

        @pl.when(phase == stride)
        def _():
            early = operands(level, stride)
            for copy in early:
                copy.start()
            inv_ref[1] = invert(d_now[...])
            middle = inverse_copies(level, stride)
            for copy in middle:
                copy.start()
            q_diag, q_rhs = right_part(inv_ref[1], u_now[...], rec_ref[1])
            q_out[...] = q_diag
            s_out[...] = q_rhs
            late = right_copies(level, stride)
            for copy in late:
                copy.start()
            for copy in early + middle + late:
                copy.wait_send()

        @pl.when(phase == 0)
        def _():
            for copy in right_copies(level, stride):
                copy.wait_recv()
            mirror(q_in.at[level - 1])
            d_now[...] -= q_in[level - 1]
            rec_ref[1] -= s_in[level - 1]
            complete(level, stride, u_now)

    @pl.when(lax.rem(me + 1, 2 ** (LEVELS - 1)) == 0)
    def _():
        inv_ref[1] = invert(d_now[...])

    for copy in operands(0, 1) + inverse_copies(0, 1):
        copy.wait_send()


def body(diag_block, coupling, right_side):
    orbitals, columns = right_side.shape[1:]
    tiles = orbitals // TILE
    square, side = (orbitals, orbitals), (orbitals, columns)
    slots = 3 + 2 * tiles
    vmem = pl.BlockSpec(memory_space=pltpu.VMEM)
    return pl.pallas_call(
        functools.partial(kernel, lax.axis_size("layer")),
        out_shape=(
            jax.ShapeDtypeStruct(diag_block.shape, jnp.float32),
            jax.ShapeDtypeStruct(right_side.shape, jnp.float32),
        ),
        in_specs=[vmem] * 3,
        out_specs=(vmem, vmem),
        scratch_shapes=[
            pltpu.VMEM(square, jnp.float32),
            pltpu.VMEM(square, jnp.float32),
            pltpu.VMEM((LEVELS,) + square, jnp.float32),
            pltpu.VMEM((LEVELS - 1,) + square, jnp.float32),
            pltpu.VMEM((LEVELS,) + side, jnp.float32),
            pltpu.VMEM(square, jnp.float32),
            pltpu.VMEM((LEVELS - 1,) + square, jnp.float32),
            pltpu.VMEM(side, jnp.float32),
            pltpu.VMEM((LEVELS - 1,) + side, jnp.float32),
            pltpu.SemaphoreType.DMA((LEVELS, slots)),
            pltpu.SemaphoreType.DMA((LEVELS, slots)),
        ],
        compiler_params=pltpu.CompilerParams(
            collective_id=0, has_side_effects=True, vmem_limit_bytes=48 * 2 ** 20
        ),
    )(diag_block, coupling, right_side)


def solution(mesh):
    return jax.shard_map(
        body,
        mesh=mesh,
        in_specs=(P("layer", None, None), P("layer", None, None), P("layer", None, "rhs")),
        out_specs=(P("layer", None, None), P("layer", None, "rhs")),
        check_vma=False,
    )
```

time: 145 us -> 58.9 us (0.41)
  waiting for transfers between devices: 53.7 us -> 0 us
  Pallas kernels: 0 us -> 52.8 us
  starting transfers between devices: 43.1 us -> 0 us
  local copies, waits for them, and re-layouts: 20.6 us -> 5.29 us
  other arithmetic: 13.1 us -> 0 us
  matrix products: 11.7 us -> 0 us
    ppermute x11 -> x0, waiting for transfers between devices: 53.7 us -> none  [passed_along(): return lax.ppermute(block, axis, route)]
    pallas_call x0 -> x1, Pallas kernels: none -> 52.8 us  [body(): pl.pallas_call(functools.partial(kernel, lax.axis_size('layer')), out_sha...]
    ppermute x11 -> x0, starting transfers between devices: 43.1 us -> none  [passed_along(): return lax.ppermute(block, axis, route)]
    dot_general x12 -> x0, matrix products: 11.7 us -> none  [matmul(): jnp.dot(first, second, precision=lax.Precision.HIGH, preferred_element_ty...]
    slice x9 -> x0, local copies, waits for them, and re-layouts: 6.48 us -> none  [the longest x3 4.1 us: send_down(): head = left_part[:, :columns]]
    select_n x6 -> x0, other arithmetic: 5.29 us -> none  [the longest x1 1.75 us: body(): jnp.where(survive, -head_in[:, orbitals:2 * orbitals], high_coup)]
    another operation x8 -> x0, local copies, waits for them, and re-layouts: 5.03 us -> none
    another operation x4 -> x0, other arithmetic: 3.94 us -> none  [the longest x2 2.76 us: body(): rhs_out = jnp.stack([low_rhs, high_record], axis=0)]
  transfers between devices with their start and end apart: 11 -> 0, of which waited for: 8 -> 0; matrix products, arithmetic and copies ran while one was open for 10% -> 0% of each run, Pallas kernels for 0% -> 0%
where the time goes in v1:
time: 58.9 us; the launch traced here: 58.7 us
  Pallas kernels  52.8 us (90%)
  local copies, waits for them, and re-layouts  5.29 us (9%)
  between operations  0.65 us (1%)
    pallas_call x1, Pallas kernels, body(): pl.pallas_call(functools.partial(kernel, lax.axis_size('layer')), out_sha...  52.8 us
    unnamed x8, local copies, waits for them, and re-layouts  5.29 us

profile of v1, /device:TPU:5, one launch (start us, length us, event | category | flops | bytes accessed | tf_op | source)
XLA Modules:
  0.0 58.7 jit_solution(3997012226498231652)
XLA Ops:
  0.6 0.0 copy-start
  0.6 1.3 %copy-done = f32[2,384,384]{2,1,0:T(8,128)S(1)} copy-done((f32[2,384,384]{2,1,0:T(8,128)S(1)}, f32[2,384,384]{2,1,0:T(8,128)}, u32[]{:S(2)}) %copy-start) | copy-done | bytes 1179672
  1.9 0.0 copy-start.1
  1.9 1.3 %copy-done.1 = f32[2,384,384]{2,1,0:T(8,128)S(1)} copy-done((f32[2,384,384]{2,1,0:T(8,128)S(1)}, f32[2,384,384]{2,1,0:T(8,128)}, u32[]{:S(2)}) %copy-start.1) | copy-done | bytes 1179672
  3.2 0.0 copy-start.2
  3.2 1.0 %copy-done.2 = f32[2,384,128]{2,1,0:T(8,128)S(1)} copy-done((f32[2,384,128]{2,1,0:T(8,128)S(1)}, f32[2,384,128]{2,1,0:T(8,128)}, u32[]{:S(2)}) %copy-start.2) | copy-done | bytes 393240
  4.2 52.8 %shard_map.50 = (f32[2,384,384]{2,1,0:T(8,128)S(1)}, f32[2,384,128]{2,1,0:T(8,128)S(1)}) custom-call(f32[2,384,384]{2,1,0:T(8,128)S(1)} %copy-done, f32[2,384,384]{2,1,0:T(8,128)S(1)} %copy-done.1, f32[2,384,128]{2,1,0:T(8,128)S(1)} %copy-done.2), custom_call_target="tpu_custom_call" | custom-call | tf_op jit(solution)/shard_map/pallas_call | solution.py:172
  56.9 1.0 %copy.7 = f32[2,384,384]{2,1,0:T(8,128)} copy(f32[2,384,384]{2,1,0:T(8,128)S(1)} %get-tuple-element.4) | data formatting | bytes 2359296
  58.0 0.7 %copy.8 = f32[2,384,128]{2,1,0:T(8,128)} copy(f32[2,384,128]{2,1,0:T(8,128)S(1)} %get-tuple-element.5) | data formatting | bytes 786432
Async XLA Ops:
  0.6 1.3 %copy-start = (f32[2,384,384]{2,1,0:T(8,128)S(1)}, f32[2,384,384]{2,1,0:T(8,128)}, u32[]{:S(2)}) copy-start(f32[2,384,384]{2,1,0:T(8,128)} %d_ref.1) | copy-start | bytes 3538948
  1.9 1.3 %copy-start.1 = (f32[2,384,384]{2,1,0:T(8,128)S(1)}, f32[2,384,384]{2,1,0:T(8,128)}, u32[]{:S(2)}) copy-start(f32[2,384,384]{2,1,0:T(8,128)} %u_ref.1) | copy-start | bytes 3538948
  3.2 1.0 %copy-start.2 = (f32[2,384,128]{2,1,0:T(8,128)S(1)}, f32[2,384,128]{2,1,0:T(8,128)}, u32[]{:S(2)}) copy-start(f32[2,384,128]{2,1,0:T(8,128)} %r_ref.1) | copy-start | bytes 1179652

commit v2 on v1

--- a/solution.py
+++ b/solution.py
@@ -42,21 +42,27 @@
     return scale * (identity + (rest + (fourth + matmul(split(rest), split(fourth)))))
 
 
-def kernel(size, d_ref, u_ref, r_ref, inv_ref, rec_ref, d_now, u_now, x_in, u_in, r_in,
-           q_out, q_in, s_out, s_in, send_sem, recv_sem):
+def kernel(size, ways, d_ref, u_ref, r_ref, inv_ref, rec_ref, d_now, u_now, x_in, u_in, r_in,
+           q_out, q_in, s_out, s_in, send_sem, recv_sem, pass_sem):
     me = lax.axis_index("layer")
+    side = lax.axis_index("rhs")
     orbitals = d_ref.shape[1]
     tiles = orbitals // TILE
 
     def at(distance):
         return {"layer": lax.rem(me + distance + size, size)}
+
+    def across(hop):
+        return {"rhs": lax.rem(side + hop, ways)}
 
     strides = [2 ** level for level in range(LEVELS - 1)]
     partners = [sign * stride for stride in strides for sign in (1, -1)]
     barrier = pltpu.get_barrier_semaphore()
     for distance in partners:
         pl.semaphore_signal(barrier, inc=1, device_id=at(distance), device_id_type=pl.DeviceIdType.MESH)
-    pl.semaphore_wait(barrier, len(partners))
+    for hop in range(1, ways):
+        pl.semaphore_signal(barrier, inc=1, device_id=across(hop), device_id_type=pl.DeviceIdType.MESH)
+    pl.semaphore_wait(barrier, len(partners) + ways - 1)
 
     def remote(src, dst, level, slot, distance):
         return pltpu.make_async_remote_copy(
@@ -65,33 +71,85 @@
             device_id_type=pl.DeviceIdType.MESH,
         )
 
-    def triangle(src, dst, level, slot, distance):
-        copies = []
+    def triangle(src, dst, slot):
+        pieces = []
         for i in range(tiles):
             part = (pl.ds(i * TILE, TILE), pl.ds(i * TILE, orbitals - i * TILE))
-            copies.append(remote(src.at[part], dst.at[part], level, slot + i, distance))
-        return copies
+            pieces.append((src.at[part], dst.at[part], slot + i, min(i, ways - 1)))
+        return pieces
+
+    def bands(src, dst, slot):
+        rows = orbitals // ways
+        parts = [pl.ds(i * rows, rows) for i in range(ways)]
+        return [(src.at[part], dst.at[part], slot + i, i) for i, part in enumerate(parts)]
+
+    def u_pieces(level):
+        return bands(u_ref.at[0] if level == 0 else u_now, u_in.at[level], 2 + 2 * tiles)
+
+    def x_pieces(level):
+        return triangle(inv_ref.at[min(level, 1)], x_in.at[level], 1)
+
+    def q_pieces(level):
+        return triangle(q_out, q_in.at[level - 1], 1 + tiles)
+
+    def r_copy(level, stride):
+        src = r_ref.at[0] if level == 0 else rec_ref.at[1]
+        return remote(src, r_in.at[level], level, 0, -stride)
+
+    def s_copy(level, stride):
+        return remote(s_out, s_in.at[level - 1], level, 1 + 2 * tiles, stride)
+
+    def mine(owner, whole):
+        return jnp.logical_or(side == owner, whole)
+
+    def give(pieces, level, distance, whole):
+        for src, dst, slot, owner in pieces:
+            @pl.when(mine(owner, whole))
+            def _():
+                remote(src, dst, level, slot, distance).start()
+
+    def given(pieces, level, distance, whole):
+        for src, dst, slot, owner in pieces:
+            @pl.when(mine(owner, whole))
+            def _():
+                remote(src, dst, level, slot, distance).wait_send()
+
+    def passing(dst, level, slot, hop):
+        return pltpu.make_async_remote_copy(
+            src_ref=dst, dst_ref=dst, send_sem=pass_sem.at[level, slot, hop - 1],
+            recv_sem=recv_sem.at[level, slot], device_id=across(hop),
+            device_id_type=pl.DeviceIdType.MESH,
+        )
+
+    def relays(owner, whole):
+        return jnp.logical_and(side == owner, jnp.logical_not(whole))
+
+    def relay(pieces, level, whole):
+        for src, dst, slot, owner in pieces:
+            @pl.when(relays(owner, whole))
+            def _():
+                remote(src, dst, level, slot, 1).wait_recv()
+                for hop in range(1, ways):
+                    passing(dst, level, slot, hop).start()
+
+    def take(pieces, level, whole):
+        for src, dst, slot, owner in pieces:
+            @pl.when(jnp.logical_not(relays(owner, whole)))
+            def _():
+                remote(src, dst, level, slot, 1).wait_recv()
+
+    def relayed(pieces, level, whole):
+        for src, dst, slot, owner in pieces:
+            @pl.when(relays(owner, whole))
+            def _():
+                for hop in range(1, ways):
+                    passing(dst, level, slot, hop).wait_send()
 
     def mirror(ref):
         for i in range(tiles):
             for j in range(i + 1, tiles):
                 low, high = pl.ds(i * TILE, TILE), pl.ds(j * TILE, TILE)
                 ref[high, low] = ref[low, high].T
-
-    def operands(level, stride):
-        src_u, src_r = (u_ref.at[0], r_ref.at[0]) if level == 0 else (u_now, rec_ref.at[1])
-        copies = [remote(src_r, r_in.at[level], level, 1, -stride)]
-        if level < LEVELS - 1:
-            copies.append(remote(src_u, u_in.at[level], level, 0, -stride))
-        return copies
-
-    def inverse_copies(level, stride):
-        return triangle(inv_ref.at[min(level, 1)], x_in.at[level], level, 2, -stride)
-
-    def right_copies(level, stride):
-        return triangle(q_out, q_in.at[level - 1], level, 2 + tiles, stride) + [
-            remote(s_out, s_in.at[level - 1], level, 2 + 2 * tiles, stride)
-        ]
 
     def right_part(approx, u_self, r_self):
         parts = split(approx)
@@ -101,9 +159,15 @@
             matmul(turned, split(matmul(parts, split(r_self)))),
         )
 
-    def complete(level, stride, u_left):
-        for copy in operands(level, stride) + inverse_copies(level, stride):
-            copy.wait_recv()
+    def complete(level, stride, u_left, whole):
+        last = level == LEVELS - 1
+        if not last and level > 0:
+            relay(u_pieces(level), level, whole)
+        relay(x_pieces(level), level, whole)
+        r_copy(level, stride).wait_recv()
+        if not last:
+            take(u_pieces(level), level, whole)
+        take(x_pieces(level), level, whole)
         mirror(x_in.at[level])
         left = split(u_left[...])
         through = split(matmul(left, split(x_in[level])))
@@ -112,65 +176,79 @@
         if level < LEVELS - 1:
             u_now[...] = -matmul(through, split(u_in[level]))
 
-    first_level = operands(0, 1)
-    for copy in first_level:
-        copy.start()
+    whole_out = lax.rem(me, 2) == 1
+    whole_in = lax.rem(me, 2) == 0
+    r_copy(0, 1).start()
+    give(u_pieces(0), 0, -1, whole_out)
     rec_ref[0] = r_ref[0]
     inv_ref[0] = invert(d_ref[0])
-    for copy in inverse_copies(0, 1):
-        copy.start()
+    give(x_pieces(0), 0, -1, whole_out)
+    relay(u_pieces(0), 0, whole_in)
     q_diag, q_rhs = right_part(inv_ref[0], u_ref[0], r_ref[0])
     d_now[...] = d_ref[1] - q_diag
     rec_ref[1] = r_ref[1] - q_rhs
-    complete(0, 1, u_ref.at[1])
+    complete(0, 1, u_ref.at[1], whole_in)
 
     for level in range(1, LEVELS):
         stride = 2 ** (level - 1)
         phase = lax.rem(me + 1, 2 * stride)
+        last = level == LEVELS - 1
+        whole_q = lax.rem(me, 1) == (0 if level == 1 else 1)
+        split_l = lax.rem(me, 1) == 1
 
         @pl.when(phase == stride)
         def _():
-            early = operands(level, stride)
-            for copy in early:
-                copy.start()
+            r_copy(level, stride).start()
+            if not last:
+                give(u_pieces(level), level, -stride, split_l)
             inv_ref[1] = invert(d_now[...])
-            middle = inverse_copies(level, stride)
-            for copy in middle:
-                copy.start()
+            give(x_pieces(level), level, -stride, split_l)
             q_diag, q_rhs = right_part(inv_ref[1], u_now[...], rec_ref[1])
             q_out[...] = q_diag
             s_out[...] = q_rhs
-            late = right_copies(level, stride)
-            for copy in late:
-                copy.start()
-            for copy in early + middle + late:
-                copy.wait_send()
+            give(q_pieces(level), level, stride, whole_q)
+            s_copy(level, stride).start()
+            r_copy(level, stride).wait_send()
+            if not last:
+                given(u_pieces(level), level, -stride, split_l)
+            given(x_pieces(level), level, -stride, split_l)
+            given(q_pieces(level), level, stride, whole_q)
+            s_copy(level, stride).wait_send()
 
         @pl.when(phase == 0)
         def _():
-            for copy in right_copies(level, stride):
-                copy.wait_recv()
+            complete(level, stride, u_now, split_l)
+            relay(q_pieces(level), level, whole_q)
+            take(q_pieces(level), level, whole_q)
+            s_copy(level, stride).wait_recv()
             mirror(q_in.at[level - 1])
             d_now[...] -= q_in[level - 1]
             rec_ref[1] -= s_in[level - 1]
-            complete(level, stride, u_now)
+            if not last:
+                relayed(u_pieces(level), level, split_l)
+            relayed(x_pieces(level), level, split_l)
+            relayed(q_pieces(level), level, whole_q)
 
     @pl.when(lax.rem(me + 1, 2 ** (LEVELS - 1)) == 0)
     def _():
         inv_ref[1] = invert(d_now[...])
 
-    for copy in operands(0, 1) + inverse_copies(0, 1):
-        copy.wait_send()
+    r_copy(0, 1).wait_send()
+    given(u_pieces(0), 0, -1, whole_out)
+    given(x_pieces(0), 0, -1, whole_out)
+    relayed(u_pieces(0), 0, whole_in)
+    relayed(x_pieces(0), 0, whole_in)
 
 
 def body(diag_block, coupling, right_side):
     orbitals, columns = right_side.shape[1:]
     tiles = orbitals // TILE
     square, side = (orbitals, orbitals), (orbitals, columns)
-    slots = 3 + 2 * tiles
+    ways = lax.axis_size("rhs")
+    slots = 2 + 2 * tiles + ways
     vmem = pl.BlockSpec(memory_space=pltpu.VMEM)
     return pl.pallas_call(
-        functools.partial(kernel, lax.axis_size("layer")),
+        functools.partial(kernel, lax.axis_size("layer"), ways),
         out_shape=(
             jax.ShapeDtypeStruct(diag_block.shape, jnp.float32),
             jax.ShapeDtypeStruct(right_side.shape, jnp.float32),
@@ -189,6 +267,7 @@
             pltpu.VMEM((LEVELS - 1,) + side, jnp.float32),
             pltpu.SemaphoreType.DMA((LEVELS, slots)),
             pltpu.SemaphoreType.DMA((LEVELS, slots)),
+            pltpu.SemaphoreType.DMA((LEVELS, slots, max(1, ways - 1))),
         ],
         compiler_params=pltpu.CompilerParams(
             collective_id=0, has_side_effects=True, vmem_limit_bytes=48 * 2 ** 20

time: 58.9 us -> 55.3 us (0.939)
  Pallas kernels: 52.8 us -> 49.1 us
    pallas_call x1, Pallas kernels: 52.8 us -> 49.1 us  [body(): pl.pallas_call(functools.partial(kernel, lax.axis_size('layer'), ways), o...]
where the time goes in v2:
time: 55.3 us; the launch traced here: 55 us
  Pallas kernels  49.1 us (89%)
  local copies, waits for them, and re-layouts  5.29 us (10%)
  between operations  0.65 us (1%)
    pallas_call x1, Pallas kernels, body(): pl.pallas_call(functools.partial(kernel, lax.axis_size('layer'), ways), o...  49.1 us
    unnamed x8, local copies, waits for them, and re-layouts  5.29 us

profile of v2, /device:TPU:5, one launch (start us, length us, event | category | flops | bytes accessed | tf_op | source)
XLA Modules:
  0.0 55.0 jit_solution(11945364718374811395)
XLA Ops:
  0.6 0.0 copy-start
  0.6 1.3 %copy-done = f32[2,384,384]{2,1,0:T(8,128)S(1)} copy-done((f32[2,384,384]{2,1,0:T(8,128)S(1)}, f32[2,384,384]{2,1,0:T(8,128)}, u32[]{:S(2)}) %copy-start) | copy-done | bytes 1179672
  1.9 0.0 copy-start.1
  1.9 1.3 %copy-done.1 = f32[2,384,384]{2,1,0:T(8,128)S(1)} copy-done((f32[2,384,384]{2,1,0:T(8,128)S(1)}, f32[2,384,384]{2,1,0:T(8,128)}, u32[]{:S(2)}) %copy-start.1) | copy-done | bytes 1179672
  3.2 0.0 copy-start.2
  3.2 1.0 %copy-done.2 = f32[2,384,128]{2,1,0:T(8,128)S(1)} copy-done((f32[2,384,128]{2,1,0:T(8,128)S(1)}, f32[2,384,128]{2,1,0:T(8,128)}, u32[]{:S(2)}) %copy-start.2) | copy-done | bytes 393240
  4.2 49.1 %shard_map.50 = (f32[2,384,384]{2,1,0:T(8,128)S(1)}, f32[2,384,128]{2,1,0:T(8,128)S(1)}) custom-call(f32[2,384,384]{2,1,0:T(8,128)S(1)} %copy-done, f32[2,384,384]{2,1,0:T(8,128)S(1)} %copy-done.1, f32[2,384,128]{2,1,0:T(8,128)S(1)} %copy-done.2), custom_call_target="tpu_custom_call" | custom-call | tf_op jit(solution)/shard_map/pallas_call | solution.py:250
  53.3 1.0 %copy.7 = f32[2,384,384]{2,1,0:T(8,128)} copy(f32[2,384,384]{2,1,0:T(8,128)S(1)} %get-tuple-element.4) | data formatting | bytes 2359296
  54.3 0.7 %copy.8 = f32[2,384,128]{2,1,0:T(8,128)} copy(f32[2,384,128]{2,1,0:T(8,128)S(1)} %get-tuple-element.5) | data formatting | bytes 786432
Async XLA Ops:
  0.6 1.3 %copy-start = (f32[2,384,384]{2,1,0:T(8,128)S(1)}, f32[2,384,384]{2,1,0:T(8,128)}, u32[]{:S(2)}) copy-start(f32[2,384,384]{2,1,0:T(8,128)} %d_ref.1) | copy-start | bytes 3538948
  1.9 1.3 %copy-start.1 = (f32[2,384,384]{2,1,0:T(8,128)S(1)}, f32[2,384,384]{2,1,0:T(8,128)}, u32[]{:S(2)}) copy-start(f32[2,384,384]{2,1,0:T(8,128)} %u_ref.1) | copy-start | bytes 3538948
  3.2 1.0 %copy-start.2 = (f32[2,384,128]{2,1,0:T(8,128)S(1)}, f32[2,384,128]{2,1,0:T(8,128)}, u32[]{:S(2)}) copy-start(f32[2,384,128]{2,1,0:T(8,128)} %r_ref.1) | copy-start | bytes 1179652

commit v3 on v2

--- a/solution.py
+++ b/solution.py
@@ -23,6 +23,10 @@
         return lax.dot_general(a, b, dims, preferred_element_type=jnp.float32)
 
     return one(first[0], second[0]) + (one(first[0], second[1]) + one(first[1], second[0]))
+
+
+def beside(first, second):
+    return tuple(jnp.concatenate(pair, axis=1) for pair in zip(first, second))
 
 
 def invert(block):
@@ -37,8 +41,9 @@
     err_parts = split(err)
     square = matmul(err_parts, err_parts)
     square_parts = split(square)
-    rest = err + (square + matmul(err_parts, square_parts))
-    fourth = matmul(square_parts, square_parts)
+    both = matmul(square_parts, beside(err_parts, square_parts))
+    rest = err + (square + both[:, :orbitals])
+    fourth = both[:, orbitals:]
     return scale * (identity + (rest + (fourth + matmul(split(rest), split(fourth)))))
 
 
@@ -154,10 +159,9 @@
     def right_part(approx, u_self, r_self):
         parts = split(approx)
         turned = split(u_self.T)
-        return (
-            matmul(turned, split(matmul(parts, split(u_self)))),
-            matmul(turned, split(matmul(parts, split(r_self)))),
-        )
+        solved = matmul(parts, beside(split(u_self), split(r_self)))
+        reduced = matmul(turned, split(solved))
+        return reduced[:, :orbitals], reduced[:, orbitals:]
 
     def complete(level, stride, u_left, whole):
         last = level == LEVELS - 1
@@ -172,9 +176,12 @@
         left = split(u_left[...])
         through = split(matmul(left, split(x_in[level])))
         d_now[...] -= matmul(through, left, transposed=True)
-        rec_ref[1] -= matmul(through, split(r_in[level]))
-        if level < LEVELS - 1:
-            u_now[...] = -matmul(through, split(u_in[level]))
+        if last:
+            rec_ref[1] -= matmul(through, split(r_in[level]))
+        else:
+            left_part = matmul(through, beside(split(u_in[level]), split(r_in[level])))
+            u_now[...] = -left_part[:, :orbitals]
+            rec_ref[1] -= left_part[:, orbitals:]
 
     whole_out = lax.rem(me, 2) == 1
     whole_in = lax.rem(me, 2) == 0

time: 55.3 us -> 55.6 us (level)
  no operation moved by 1% of the time
where the time goes in v3:
time: 55.6 us; the launch traced here: 55.4 us
  Pallas kernels  49.4 us (89%)
  local copies, waits for them, and re-layouts  5.29 us (10%)
  between operations  0.65 us (1%)
    pallas_call x1, Pallas kernels, body(): pl.pallas_call(functools.partial(kernel, lax.axis_size('layer'), ways), o...  49.4 us
    unnamed x8, local copies, waits for them, and re-layouts  5.29 us

profile of v3, /device:TPU:5, one launch (start us, length us, event | category | flops | bytes accessed | tf_op | source)
XLA Modules:
  0.0 55.4 jit_solution(13815472460391626236)
XLA Ops:
  0.6 0.0 copy-start
  0.6 1.3 %copy-done = f32[2,384,384]{2,1,0:T(8,128)S(1)} copy-done((f32[2,384,384]{2,1,0:T(8,128)S(1)}, f32[2,384,384]{2,1,0:T(8,128)}, u32[]{:S(2)}) %copy-start) | copy-done | bytes 1179672
  1.9 0.0 copy-start.1
  1.9 1.3 %copy-done.1 = f32[2,384,384]{2,1,0:T(8,128)S(1)} copy-done((f32[2,384,384]{2,1,0:T(8,128)S(1)}, f32[2,384,384]{2,1,0:T(8,128)}, u32[]{:S(2)}) %copy-start.1) | copy-done | bytes 1179672
  3.2 0.0 copy-start.2
  3.2 1.0 %copy-done.2 = f32[2,384,128]{2,1,0:T(8,128)S(1)} copy-done((f32[2,384,128]{2,1,0:T(8,128)S(1)}, f32[2,384,128]{2,1,0:T(8,128)}, u32[]{:S(2)}) %copy-start.2) | copy-done | bytes 393240
  4.2 49.4 %shard_map.50 = (f32[2,384,384]{2,1,0:T(8,128)S(1)}, f32[2,384,128]{2,1,0:T(8,128)S(1)}) custom-call(f32[2,384,384]{2,1,0:T(8,128)S(1)} %copy-done, f32[2,384,384]{2,1,0:T(8,128)S(1)} %copy-done.1, f32[2,384,128]{2,1,0:T(8,128)S(1)} %copy-done.2), custom_call_target="tpu_custom_call" | custom-call | tf_op jit(solution)/shard_map/pallas_call | solution.py:257
  53.6 1.0 %copy.7 = f32[2,384,384]{2,1,0:T(8,128)} copy(f32[2,384,384]{2,1,0:T(8,128)S(1)} %get-tuple-element.4) | data formatting | bytes 2359296
  54.6 0.7 %copy.8 = f32[2,384,128]{2,1,0:T(8,128)} copy(f32[2,384,128]{2,1,0:T(8,128)S(1)} %get-tuple-element.5) | data formatting | bytes 786432
Async XLA Ops:
  0.6 1.3 %copy-start = (f32[2,384,384]{2,1,0:T(8,128)S(1)}, f32[2,384,384]{2,1,0:T(8,128)}, u32[]{:S(2)}) copy-start(f32[2,384,384]{2,1,0:T(8,128)} %d_ref.1) | copy-start | bytes 3538948
  1.9 1.3 %copy-start.1 = (f32[2,384,384]{2,1,0:T(8,128)S(1)}, f32[2,384,384]{2,1,0:T(8,128)}, u32[]{:S(2)}) copy-start(f32[2,384,384]{2,1,0:T(8,128)} %u_ref.1) | copy-start | bytes 3538948
  3.2 1.0 %copy-start.2 = (f32[2,384,128]{2,1,0:T(8,128)S(1)}, f32[2,384,128]{2,1,0:T(8,128)}, u32[]{:S(2)}) copy-start(f32[2,384,128]{2,1,0:T(8,128)} %r_ref.1) | copy-start | bytes 1179652

commit v4 on v3

--- a/solution.py
+++ b/solution.py
@@ -168,14 +168,14 @@
         if not last and level > 0:
             relay(u_pieces(level), level, whole)
         relay(x_pieces(level), level, whole)
-        r_copy(level, stride).wait_recv()
-        if not last:
-            take(u_pieces(level), level, whole)
         take(x_pieces(level), level, whole)
         mirror(x_in.at[level])
         left = split(u_left[...])
         through = split(matmul(left, split(x_in[level])))
         d_now[...] -= matmul(through, left, transposed=True)
+        if not last:
+            take(u_pieces(level), level, whole)
+        r_copy(level, stride).wait_recv()
         if last:
             rec_ref[1] -= matmul(through, split(r_in[level]))
         else:
@@ -185,11 +185,11 @@
 
     whole_out = lax.rem(me, 2) == 1
     whole_in = lax.rem(me, 2) == 0
-    r_copy(0, 1).start()
     give(u_pieces(0), 0, -1, whole_out)
     rec_ref[0] = r_ref[0]
     inv_ref[0] = invert(d_ref[0])
     give(x_pieces(0), 0, -1, whole_out)
+    r_copy(0, 1).start()
     relay(u_pieces(0), 0, whole_in)
     q_diag, q_rhs = right_part(inv_ref[0], u_ref[0], r_ref[0])
     d_now[...] = d_ref[1] - q_diag
@@ -205,11 +205,14 @@
 
         @pl.when(phase == stride)
         def _():
-            r_copy(level, stride).start()
-            if not last:
+            if last:
+                r_copy(level, stride).start()
+            else:
                 give(u_pieces(level), level, -stride, split_l)
             inv_ref[1] = invert(d_now[...])
             give(x_pieces(level), level, -stride, split_l)
+            if not last:
+                r_copy(level, stride).start()
             q_diag, q_rhs = right_part(inv_ref[1], u_now[...], rec_ref[1])
             q_out[...] = q_diag
             s_out[...] = q_rhs

time: 55.6 us -> 54.2 us (0.975)
  Pallas kernels: 49.4 us -> 48 us
    pallas_call x1, Pallas kernels: 49.4 us -> 48 us  [body(): pl.pallas_call(functools.partial(kernel, lax.axis_size('layer'), ways), o...]
where the time goes in v4:
time: 54.2 us; the launch traced here: 53.9 us
  Pallas kernels  48 us (89%)
  local copies, waits for them, and re-layouts  5.29 us (10%)
  between operations  0.65 us (1%)
    pallas_call x1, Pallas kernels, body(): pl.pallas_call(functools.partial(kernel, lax.axis_size('layer'), ways), o...  48 us
    unnamed x8, local copies, waits for them, and re-layouts  5.29 us

profile of v4, /device:TPU:5, one launch (start us, length us, event | category | flops | bytes accessed | tf_op | source)
XLA Modules:
  0.0 53.9 jit_solution(11769240767002993642)
XLA Ops:
  0.6 0.0 copy-start
  0.6 1.3 %copy-done = f32[2,384,384]{2,1,0:T(8,128)S(1)} copy-done((f32[2,384,384]{2,1,0:T(8,128)S(1)}, f32[2,384,384]{2,1,0:T(8,128)}, u32[]{:S(2)}) %copy-start) | copy-done | bytes 1179672
  1.9 0.0 copy-start.1
  1.9 1.3 %copy-done.1 = f32[2,384,384]{2,1,0:T(8,128)S(1)} copy-done((f32[2,384,384]{2,1,0:T(8,128)S(1)}, f32[2,384,384]{2,1,0:T(8,128)}, u32[]{:S(2)}) %copy-start.1) | copy-done | bytes 1179672
  3.2 0.0 copy-start.2
  3.2 1.0 %copy-done.2 = f32[2,384,128]{2,1,0:T(8,128)S(1)} copy-done((f32[2,384,128]{2,1,0:T(8,128)S(1)}, f32[2,384,128]{2,1,0:T(8,128)}, u32[]{:S(2)}) %copy-start.2) | copy-done | bytes 393240
  4.2 48.0 %shard_map.50 = (f32[2,384,384]{2,1,0:T(8,128)S(1)}, f32[2,384,128]{2,1,0:T(8,128)S(1)}) custom-call(f32[2,384,384]{2,1,0:T(8,128)S(1)} %copy-done, f32[2,384,384]{2,1,0:T(8,128)S(1)} %copy-done.1, f32[2,384,128]{2,1,0:T(8,128)S(1)} %copy-done.2), custom_call_target="tpu_custom_call" | custom-call | tf_op jit(solution)/shard_map/pallas_call | solution.py:260
  52.2 1.0 %copy.7 = f32[2,384,384]{2,1,0:T(8,128)} copy(f32[2,384,384]{2,1,0:T(8,128)S(1)} %get-tuple-element.4) | data formatting | bytes 2359296
  53.2 0.7 %copy.8 = f32[2,384,128]{2,1,0:T(8,128)} copy(f32[2,384,128]{2,1,0:T(8,128)S(1)} %get-tuple-element.5) | data formatting | bytes 786432
Async XLA Ops:
  0.6 1.3 %copy-start = (f32[2,384,384]{2,1,0:T(8,128)S(1)}, f32[2,384,384]{2,1,0:T(8,128)}, u32[]{:S(2)}) copy-start(f32[2,384,384]{2,1,0:T(8,128)} %d_ref.1) | copy-start | bytes 3538948
  1.9 1.3 %copy-start.1 = (f32[2,384,384]{2,1,0:T(8,128)S(1)}, f32[2,384,384]{2,1,0:T(8,128)}, u32[]{:S(2)}) copy-start(f32[2,384,384]{2,1,0:T(8,128)} %u_ref.1) | copy-start | bytes 3538948
  3.2 1.0 %copy-start.2 = (f32[2,384,128]{2,1,0:T(8,128)S(1)}, f32[2,384,128]{2,1,0:T(8,128)}, u32[]{:S(2)}) copy-start(f32[2,384,128]{2,1,0:T(8,128)} %r_ref.1) | copy-start | bytes 1179652

commit v5 on v4

--- a/solution.py
+++ b/solution.py
@@ -200,7 +200,7 @@
         stride = 2 ** (level - 1)
         phase = lax.rem(me + 1, 2 * stride)
         last = level == LEVELS - 1
-        whole_q = lax.rem(me, 1) == (0 if level == 1 else 1)
+        whole_q = lax.rem(me, 1) == 0
         split_l = lax.rem(me, 1) == 1
 
         @pl.when(phase == stride)

time: 54.2 us -> 50.7 us (0.935)
  Pallas kernels: 48 us -> 44.5 us
    pallas_call x1, Pallas kernels: 48 us -> 44.5 us  [body(): pl.pallas_call(functools.partial(kernel, lax.axis_size('layer'), ways), o...]
where the time goes in v5:
time: 50.7 us; the launch traced here: 50.5 us
  Pallas kernels  44.5 us (88%)
  local copies, waits for them, and re-layouts  5.29 us (10%)
  between operations  0.65 us (1%)
    pallas_call x1, Pallas kernels, body(): pl.pallas_call(functools.partial(kernel, lax.axis_size('layer'), ways), o...  44.5 us
    unnamed x8, local copies, waits for them, and re-layouts  5.29 us

profile of v5, /device:TPU:5, one launch (start us, length us, event | category | flops | bytes accessed | tf_op | source)
XLA Modules:
  0.0 50.5 jit_solution(13628578514154560003)
XLA Ops:
  0.6 0.0 copy-start
  0.6 1.3 %copy-done = f32[2,384,384]{2,1,0:T(8,128)S(1)} copy-done((f32[2,384,384]{2,1,0:T(8,128)S(1)}, f32[2,384,384]{2,1,0:T(8,128)}, u32[]{:S(2)}) %copy-start) | copy-done | bytes 1179672
  1.9 0.0 copy-start.1
  1.9 1.3 %copy-done.1 = f32[2,384,384]{2,1,0:T(8,128)S(1)} copy-done((f32[2,384,384]{2,1,0:T(8,128)S(1)}, f32[2,384,384]{2,1,0:T(8,128)}, u32[]{:S(2)}) %copy-start.1) | copy-done | bytes 1179672
  3.2 0.0 copy-start.2
  3.2 1.0 %copy-done.2 = f32[2,384,128]{2,1,0:T(8,128)S(1)} copy-done((f32[2,384,128]{2,1,0:T(8,128)S(1)}, f32[2,384,128]{2,1,0:T(8,128)}, u32[]{:S(2)}) %copy-start.2) | copy-done | bytes 393240
  4.2 44.5 %shard_map.50 = (f32[2,384,384]{2,1,0:T(8,128)S(1)}, f32[2,384,128]{2,1,0:T(8,128)S(1)}) custom-call(f32[2,384,384]{2,1,0:T(8,128)S(1)} %copy-done, f32[2,384,384]{2,1,0:T(8,128)S(1)} %copy-done.1, f32[2,384,128]{2,1,0:T(8,128)S(1)} %copy-done.2), custom_call_target="tpu_custom_call" | custom-call | tf_op jit(solution)/shard_map/pallas_call | solution.py:260
  48.7 1.0 %copy.7 = f32[2,384,384]{2,1,0:T(8,128)} copy(f32[2,384,384]{2,1,0:T(8,128)S(1)} %get-tuple-element.4) | data formatting | bytes 2359296
  49.7 0.7 %copy.8 = f32[2,384,128]{2,1,0:T(8,128)} copy(f32[2,384,128]{2,1,0:T(8,128)S(1)} %get-tuple-element.5) | data formatting | bytes 786432
Async XLA Ops:
  0.6 1.3 %copy-start = (f32[2,384,384]{2,1,0:T(8,128)S(1)}, f32[2,384,384]{2,1,0:T(8,128)}, u32[]{:S(2)}) copy-start(f32[2,384,384]{2,1,0:T(8,128)} %d_ref.1) | copy-start | bytes 3538948
  1.9 1.3 %copy-start.1 = (f32[2,384,384]{2,1,0:T(8,128)S(1)}, f32[2,384,384]{2,1,0:T(8,128)}, u32[]{:S(2)}) copy-start(f32[2,384,384]{2,1,0:T(8,128)} %u_ref.1) | copy-start | bytes 3538948
  3.2 1.0 %copy-start.2 = (f32[2,384,128]{2,1,0:T(8,128)S(1)}, f32[2,384,128]{2,1,0:T(8,128)}, u32[]{:S(2)}) copy-start(f32[2,384,128]{2,1,0:T(8,128)} %r_ref.1) | copy-start | bytes 1179652
